TPU v7x, 512 devices: a whole 4x4x16 slice. The times are simulated.
512 devices in a mesh: pipe: 16 (over z), blk: 32 (over x, y, core).
Axes of the slice: x: 4, y: 4, z: 16, core: 2. Of those that a mesh axis runs over, the one named last changes fastest.
Arguments:
- stream: bfloat16 [16, 128, 6144], P('pipe', 'blk'), may hold values from -6 to 6
- arrivals: bfloat16 [3, 128, 6144], P(None, 'blk'), may hold values from -6 to 6
- ln_gain: bfloat16 [16, 6144], P('pipe'), may hold values from 0.099609375 to 1.8984375
- ln_bias: bfloat16 [16, 6144], P('pipe'), may hold values from -3 to 3
- up_weight: bfloat16 [16, 6144, 4096], P('pipe', None, 'blk'), may hold values from -0.078125 to 0.078125
- up_bias: bfloat16 [16, 4096], P('pipe', 'blk'), may hold values from -3 to 3
- down_weight: bfloat16 [16, 4096, 6144], P('pipe', 'blk'), may hold values from -0.1875 to 0.1875
- down_bias: bfloat16 [16, 6144], P('pipe'), may hold values from -3 to 3
- active: int32 [4, 16, 2, 16], P(None, 'pipe'), may hold values from -1 to 31, as said below
Outputs:
- passed: bfloat16 [16, 4, 128, 6144], P('pipe', None, 'blk')
Inputs may be any that keep to these rules, and one draw needn't show every extreme that they name: Each list holds between 8 and 16 distinct block ids, followed by -1 padding; some blocks are active far more often than others.
All inputs are finite; a program needn't handle non-finite values.
Results may differ from a plain program's by a relative error of at most 0.019.
Values may be sent and summed in bfloat16 or wider, within the bound.
No kernel may reach another device: no remote copies, remote signals or barrier semaphores. Data moves between devices by JAX's collectives and lax.ppermute only.
A program may use at most 64 MiB of HBM per device.

v0:
```python
import jax
import jax.numpy as jnp
from jax import lax
from jax.sharding import PartitionSpec as P

TILE = 64
TICKS = 4


def shifted(block, axis, distance):
    devices = range(lax.axis_size(axis))
    route = [(i - distance, i) for i in devices if i - distance in devices]
    return lax.ppermute(block, axis, route)


def layer_norm(rows, gain_row, shift_row):
    widened = rows.astype(jnp.float32)
    row_mean = jnp.mean(widened, axis=-1, keepdims=True)
    centred = widened - row_mean
    row_var = jnp.mean(centred * centred, axis=-1, keepdims=True)
    scaled = centred * lax.rsqrt(row_var + 1e-05)
    return (scaled * gain_row + shift_row).astype(jnp.bfloat16)


def on_device(
    stream, arrivals, ln_gain, ln_bias, up_weight, up_bias, down_weight, down_bias, active
):
    blocks = lax.axis_size("blk")
    my_index = lax.axis_index("blk")
    section = lax.axis_index("pipe")
    rows_dev = stream.shape[1]
    width = stream.shape[2]
    w_up = up_weight[0]
    b_up = up_bias[0].astype(jnp.float32)
    w_down = down_weight[0]
    gain_row = ln_gain[0].astype(jnp.float32)
    shift_row = ln_bias[0].astype(jnp.float32)
    b_down = down_bias[0].astype(jnp.float32)
    current = stream[0]
    results = []
    for step_index in range(TICKS):
        tile_lists = active[step_index, 0]
        tile_count = tile_lists.shape[0]
        owned_tiles = jnp.any(tile_lists == my_index, axis=1).astype(jnp.float32)
        normed = layer_norm(current, gain_row, shift_row)
        piece = lax.all_gather(normed, "blk", axis=0, tiled=True)
        row_index = jnp.arange(piece.shape[0], dtype=jnp.int32)
        matches = row_index[:, None] // TILE == jnp.arange(tile_count, dtype=jnp.int32)[None, :]
        row_flag = jnp.sum(matches.astype(jnp.float32) * owned_tiles[None, :], axis=1)
        preact = jnp.dot(piece, w_up, preferred_element_type=jnp.float32) + b_up
        activity = (jnp.maximum(preact, 0.0) * row_flag[:, None]).astype(jnp.bfloat16)
        partials = jnp.dot(activity, w_down, preferred_element_type=jnp.float32).astype(
            jnp.bfloat16
        )
        stacked = partials.reshape(blocks, rows_dev, width)
        received = lax.all_to_all(stacked, "blk", split_axis=0, concat_axis=0, tiled=True)
        summed = jnp.sum(received.astype(jnp.float32), axis=0)
        produced = (current.astype(jnp.float32) + summed + b_down).astype(jnp.bfloat16)
        results.append(produced)
        if step_index + 1 < TICKS:
            moved = shifted(produced, "pipe", 1)
            current = jnp.where(section == 0, arrivals[step_index], moved)
    return jnp.stack(results)[None]


def solution(mesh):
    return jax.shard_map(
        on_device,
        mesh=mesh,
        in_specs=(
            P("pipe", "blk", None),
            P(None, "blk", None),
            P("pipe", None),
            P("pipe", None),
            P("pipe", None, "blk"),
            P("pipe", "blk"),
            P("pipe", "blk", None),
            P("pipe", None),
            P(None, "pipe", None, None),
        ),
        out_specs=P("pipe", None, "blk", None),
        check_vma=False,
    )
```

profile of v0, /device:TPU:1, one launch (start us, length us, event | category | flops | bytes accessed | tf_op | source)
XLA Modules:
  0.0 441.8 jit_solution(18012084157302393708)
XLA Ops:
  6.5 1.1 convert_reduce_fusion.7
  7.6 1.0 fusion.90
  10.2 1.5 fusion.105
  13.4 62.7 %all-gather.9.cloned.1.call-done = bf16[32,4,6144]{2,1,0:T(4,128)(2,1)} async-done(((bf16[1,4,6144]{2,1,0:T(4,128)(2,1)}), bf16[32,4,6144]{2,1,0:T(4,128)(2,1)}) %all-gather.9.cloned.1.call-update) | async-done | bytes 1572880 | tf_op jit(solution)/shard_map/all_gather | solution.py:46
  76.2 3.7 reshape.139
  79.9 3.6 convolution_convert_fusion.3
  83.5 3.8 reshape.130
  87.3 5.4 %all-to-all-start = ((bf16[32,4,6144]{2,1,0:T(4,128)(2,1)}), bf16[32,4,6144]{2,1,0:T(4,128)(2,1)}, u32[]{:S(2)}, u32[]{:S(2)}) async-start(bf16[32,4,6144]{2,1,0:T(4,128)(2,1)} %reshape.130), calls=%async_computation | async-start | bytes 3145728 | tf_op jit(solution)/shard_map/all_to_all | solution.py:56
  92.8 22.6 %all-to-all-done = bf16[32,4,6144]{2,1,0:T(4,128)(2,1)} async-done(((bf16[32,4,6144]{2,1,0:T(4,128)(2,1)}), bf16[32,4,6144]{2,1,0:T(4,128)(2,1)}, u32[]{:S(2)}, u32[]{:S(2)}) %all-to-all-start) | async-done | bytes 1572896 | tf_op jit(solution)/shard_map/all_to_all | solution.py:56
  115.4 2.1 convert_reduce_fusion.3
  117.6 3.2 collective-permute-start
  120.8 1.2 collective-permute-done
  123.9 59.6 %all-gather.11.cloned.1.call-done = bf16[32,4,6144]{2,1,0:T(4,128)(2,1)} async-done(((bf16[1,4,6144]{2,1,0:T(4,128)(2,1)}), bf16[32,4,6144]{2,1,0:T(4,128)(2,1)}) %all-gather.11.cloned.1.call-update) | async-done | bytes 1572880 | tf_op jit(solution)/shard_map/all_gather | solution.py:46
  183.5 3.7 reshape.141
  187.2 3.6 convolution_convert_fusion.2
  190.8 3.8 reshape.131
  194.6 28.1 %all_to_all.20 = bf16[32,4,6144]{2,1,0:T(4,128)(2,1)S(1)} all-to-all(bf16[32,4,6144]{2,1,0:T(4,128)(2,1)} %reshape.131), channel_id=1, replica_groups=mesh['pipe'=16,'blk'=32] {'blk'}, dimensions={0} | all-to-all | bytes 3145728 | tf_op jit(solution)/shard_map/all_to_all | solution.py:56
  223.4 3.2 collective-permute-start.1
  226.6 1.3 collective-permute-done.1
  229.9 59.2 %all-gather.13.cloned.1.call-done = bf16[32,4,6144]{2,1,0:T(4,128)(2,1)} async-done(((bf16[1,4,6144]{2,1,0:T(4,128)(2,1)}), bf16[32,4,6144]{2,1,0:T(4,128)(2,1)}) %all-gather.13.cloned.1.call-update) | async-done | bytes 1572880 | tf_op jit(solution)/shard_map/all_gather | solution.py:46
  289.1 3.7 reshape.143
  292.8 3.6 convolution_convert_fusion.1
  296.4 3.8 reshape.132
  300.2 28.1 %all_to_all.21 = bf16[32,4,6144]{2,1,0:T(4,128)(2,1)S(1)} all-to-all(bf16[32,4,6144]{2,1,0:T(4,128)(2,1)} %reshape.132), channel_id=1, replica_groups=mesh['pipe'=16,'blk'=32] {'blk'}, dimensions={0} | all-to-all | bytes 3145728 | tf_op jit(solution)/shard_map/all_to_all | solution.py:56
  329.0 3.2 collective-permute-start.2
  332.1 1.3 collective-permute-done.2
  335.4 59.3 %all-gather.15.cloned.1.call-done = bf16[32,4,6144]{2,1,0:T(4,128)(2,1)} async-done(((bf16[1,4,6144]{2,1,0:T(4,128)(2,1)}), bf16[32,4,6144]{2,1,0:T(4,128)(2,1)}) %all-gather.15.cloned.1.call-update) | async-done | bytes 1572880 | tf_op jit(solution)/shard_map/all_gather | solution.py:46
  394.7 3.7 reshape.145
  398.4 3.6 convolution_convert_fusion
  402.0 3.8 reshape.133
  405.8 5.2 %all-to-all-start.3 = ((bf16[32,4,6144]{2,1,0:T(4,128)(2,1)}), bf16[32,4,6144]{2,1,0:T(4,128)(2,1)S(1)}, u32[]{:S(2)}, u32[]{:S(2)}) async-start(bf16[32,4,6144]{2,1,0:T(4,128)(2,1)} %reshape.133), calls=%async_computation.3 | async-start | bytes 3145728 | tf_op jit(solution)/shard_map/all_to_all | solution.py:56
  411.1 22.6 %all-to-all-done.3 = bf16[32,4,6144]{2,1,0:T(4,128)(2,1)S(1)} async-done(((bf16[32,4,6144]{2,1,0:T(4,128)(2,1)}), bf16[32,4,6144]{2,1,0:T(4,128)(2,1)S(1)}, u32[]{:S(2)}, u32[]{:S(2)}) %all-to-all-start.3) | async-done | bytes 1572896 | tf_op jit(solution)/shard_map/all_to_all | solution.py:56
  (53 shorter events, 12.3 us)
Async XLA Ops:
  6.5 73.3 %copy-start = (bf16[1,128,6144]{2,1,0:T(8,128)(2,1)S(1)}, bf16[1,128,6144]{2,1,0:T(8,128)(2,1)}, u32[]{:S(2)}) copy-start(bf16[1,128,6144]{2,1,0:T(8,128)(2,1)} %param.15) | copy-start | bytes 4718596
  6.5 69.7 %all-gather.9.cloned.1.call-start = ((), (), s32[]{:S(2)}) async-start(), calls=%async_computation.4 | async-start | bytes 1622016 | tf_op jit(solution)/shard_map/all_gather | solution.py:46
  13.4 66.4 %copy-start.1 = (bf16[1,6144,128]{2,1,0:T(8,128)(2,1)S(1)}, bf16[1,6144,128]{2,1,0:T(8,128)(2,1)}, u32[]{:S(2)}) copy-start(bf16[1,6144,128]{2,1,0:T(8,128)(2,1)} %param.13) | copy-start | bytes 4718596
  87.3 5.5 %copy-start.3 = (bf16[1,6144]{1,0:T(2,128)(2,1)S(1)}, bf16[1,6144]{1,0:T(2,128)(2,1)}, u32[]{:S(2)}) copy-start(bf16[1,6144]{1,0:T(2,128)(2,1)} %param.16) | copy-start | bytes 36868
  87.3 28.1 %all-to-all-start = ((bf16[32,4,6144]{2,1,0:T(4,128)(2,1)}), bf16[32,4,6144]{2,1,0:T(4,128)(2,1)}, u32[]{:S(2)}, u32[]{:S(2)}) async-start(bf16[32,4,6144]{2,1,0:T(4,128)(2,1)} %reshape.130), calls=%async_computation | async-start | bytes 3145728 | tf_op jit(solution)/shard_map/all_to_all | solution.py:56
  92.7 24.8 %copy-start.2 = (bf16[1,4,6144]{2,1,0:T(4,128)(2,1)S(1)}, bf16[1,4,6144]{2,1,0:T(4,128)(2,1)}, u32[]{:S(2)}) copy-start(bf16[1,4,6144]{2,1,0:T(4,128)(2,1)} %param.9) | copy-start | bytes 147460
  92.7 90.8 %all-gather.11.cloned.1.call-start = ((), (), s32[]{:S(2)}) async-start(), calls=%async_computation.5 | async-start | bytes 1622016 | tf_op jit(solution)/shard_map/all_gather | solution.py:46
  117.6 4.3 collective-permute-start
  123.9 165.2 %all-gather.13.cloned.1.call-start = ((), (), s32[]{:S(2)}) async-start(), calls=%async_computation.6 | async-start | bytes 1622016 | tf_op jit(solution)/shard_map/all_gather | solution.py:46
  223.4 4.5 %collective-permute-start.1 = (bf16[4,6144]{1,0:T(4,128)(2,1)S(1)}, bf16[4,6144]{1,0:T(4,128)(2,1)S(1)}, u32[]{:S(2)}, u32[]{:S(2)}) collective-permute-start(bf16[4,6144]{1,0:T(4,128)(2,1)S(1)} %fusion.99), channel_id=1, source_target_pairs={{0,32},{32,64},{64,96},{96,128},{128,160},{160,192},{192,224},{224... | collective-permute-start | bytes 147464 | tf_op jit(solution)/shard_map/ppermute | solution.py:13
  229.9 164.8 %all-gather.15.cloned.1.call-start = ((), (), s32[]{:S(2)}) async-start(), calls=%async_computation.7 | async-start | bytes 1622016 | tf_op jit(solution)/shard_map/all_gather | solution.py:46
  329.0 4.5 %collective-permute-start.2 = (bf16[4,6144]{1,0:T(4,128)(2,1)S(1)}, bf16[4,6144]{1,0:T(4,128)(2,1)S(1)}, u32[]{:S(2)}, u32[]{:S(2)}) collective-permute-start(bf16[4,6144]{1,0:T(4,128)(2,1)S(1)} %fusion.101), channel_id=1, source_target_pairs={{0,32},{32,64},{64,96},{96,128},{128,160},{160,192},{192,224},{224... | collective-permute-start | bytes 147464 | tf_op jit(solution)/shard_map/ppermute | solution.py:13
  405.8 27.9 %all-to-all-start.3 = ((bf16[32,4,6144]{2,1,0:T(4,128)(2,1)}), bf16[32,4,6144]{2,1,0:T(4,128)(2,1)S(1)}, u32[]{:S(2)}, u32[]{:S(2)}) async-start(bf16[32,4,6144]{2,1,0:T(4,128)(2,1)} %reshape.133), calls=%async_computation.3 | async-start | bytes 3145728 | tf_op jit(solution)/shard_map/all_to_all | solution.py:56
Sparse Core Ops, SparseCore 0:
  11.9 64.2 all-gather.8
  124.0 59.4 all-gather.10
  230.0 59.0 all-gather.12
  335.6 59.0 all-gather.14
where the time goes:
time: 443 us; the launch traced here: 442 us
  waiting for transfers between devices  290 us (65%)
  blocking collectives  56.1 us (13%)
  local copies, waits for them, and re-layouts  29.9 us (7%)
  starting transfers between devices  20.3 us (5%)
  other arithmetic  17.7 us (4%)
  matrix products  14.5 us (3%)
  between operations  13.3 us (3%)
    all_gather x4, waiting for transfers between devices, on_device(): piece = lax.all_gather(normed, 'blk', axis=0, tiled=True)  241 us
    all_to_all x2, blocking collectives, on_device(): lax.all_to_all(stacked, 'blk', split_axis=0, concat_axis=0, tiled=True)  56.1 us
    all_to_all x2, waiting for transfers between devices, on_device(): lax.all_to_all(stacked, 'blk', split_axis=0, concat_axis=0, tiled=True)  45.3 us
    reshape x4, local copies, waits for them, and re-layouts, on_device(): stacked = partials.reshape(blocks, rows_dev, width)  15.2 us
    unnamed x12, local copies, waits for them, and re-layouts  14.7 us
    dot_general x4, matrix products, on_device(): jnp.dot(activity, w_down, preferred_element_type=jnp.float32)  14.5 us
    all_to_all x2, starting transfers between devices, on_device(): lax.all_to_all(stacked, 'blk', split_axis=0, concat_axis=0, tiled=True)  10.6 us
    ppermute x3, starting transfers between devices, shifted(): return lax.ppermute(block, axis, route)  9.54 us
  transfers between devices with their start and end apart: 9, of which 9 were waited for; matrix products, arithmetic and copies ran while one was open for 0% of the time, Pallas kernels for 0%

commit v1 on v0

--- a/solution.py
+++ b/solution.py
@@ -43,7 +43,8 @@
         tile_count = tile_lists.shape[0]
         owned_tiles = jnp.any(tile_lists == my_index, axis=1).astype(jnp.float32)
         normed = layer_norm(current, gain_row, shift_row)
-        piece = lax.all_gather(normed, "blk", axis=0, tiled=True)
+        sent = jnp.stack([normed] * lax.axis_size("blk"))
+        piece = jnp.concatenate(lax.all_to_all(sent, "blk", 0, 0), axis=0)
         row_index = jnp.arange(piece.shape[0], dtype=jnp.int32)
         matches = row_index[:, None] // TILE == jnp.arange(tile_count, dtype=jnp.int32)[None, :]
         row_flag = jnp.sum(matches.astype(jnp.float32) * owned_tiles[None, :], axis=1)

time: 443 us -> 303 us (0.68)
  waiting for transfers between devices: 290 us -> 71.5 us
  blocking collectives: 56.1 us -> 135 us
  between operations: 13.3 us -> 0.27 us
  starting transfers between devices: 20.3 us -> 29.4 us
    all_gather x4 -> x0, waiting for transfers between devices: 241 us -> none  [on_device(): piece = lax.all_gather(normed, 'blk', axis=0, tiled=True)]
    all_to_all x0 -> x3, blocking collectives: none -> 81.7 us  [on_device(): piece = jnp.concatenate(lax.all_to_all(sent, 'blk', 0, 0), axis=0)]
    all_to_all x0 -> x1, waiting for transfers between devices: none -> 22.5 us  [on_device(): piece = jnp.concatenate(lax.all_to_all(sent, 'blk', 0, 0), axis=0)]
    unnamed x12, local copies, waits for them, and re-layouts: 14.7 us -> 0.03 us
    reshape x0 -> x4, local copies, waits for them, and re-layouts: none -> 14.6 us  [on_device(): piece = jnp.concatenate(lax.all_to_all(sent, 'blk', 0, 0), axis=0)]
    all_to_all x0 -> x1, starting transfers between devices: none -> 11.3 us  [on_device(): piece = jnp.concatenate(lax.all_to_all(sent, 'blk', 0, 0), axis=0)]
  transfers between devices with their start and end apart: 9 -> 6, of which waited for: 9 -> 6; matrix products, arithmetic and copies ran while one was open for 0% -> 0% of each run, Pallas kernels for 0% -> 0%
where the time goes in v1:
time: 303 us; the launch traced here: 298 us
  blocking collectives  135 us (45%)
  waiting for transfers between devices  71.5 us (24%)
  local copies, waits for them, and re-layouts  33.8 us (11%)
  starting transfers between devices  29.4 us (10%)
  matrix products  14.5 us (5%)
  other arithmetic  13.9 us (5%)
    all_to_all x3, blocking collectives, on_device(): piece = jnp.concatenate(lax.all_to_all(sent, 'blk', 0, 0), axis=0)  81.7 us
    all_to_all x2, blocking collectives, on_device(): lax.all_to_all(stacked, 'blk', split_axis=0, concat_axis=0, tiled=True)  52.9 us
    all_to_all x2, waiting for transfers between devices, on_device(): lax.all_to_all(stacked, 'blk', split_axis=0, concat_axis=0, tiled=True)  45.3 us
    all_to_all x1, waiting for transfers between devices, on_device(): piece = jnp.concatenate(lax.all_to_all(sent, 'blk', 0, 0), axis=0)  22.5 us
    reshape x4, local copies, waits for them, and re-layouts, on_device(): stacked = partials.reshape(blocks, rows_dev, width)  15.2 us
    reshape x4, local copies, waits for them, and re-layouts, on_device(): piece = jnp.concatenate(lax.all_to_all(sent, 'blk', 0, 0), axis=0)  14.6 us
    dot_general x4, matrix products, on_device(): jnp.dot(activity, w_down, preferred_element_type=jnp.float32)  14.5 us
    all_to_all x1, starting transfers between devices, on_device(): piece = jnp.concatenate(lax.all_to_all(sent, 'blk', 0, 0), axis=0)  11.3 us
  transfers between devices with their start and end apart: 6, of which 6 were waited for; matrix products, arithmetic and copies ran while one was open for 0% of the time, Pallas kernels for 0%

profile of v1, /device:TPU:1, one launch (start us, length us, event | category | flops | bytes accessed | tf_op | source)
XLA Modules:
  0.0 298.1 jit_solution(13997418362415670369)
XLA Ops:
  0.0 1.1 convert_reduce_fusion.4
  4.6 1.9 stack.19
  6.4 11.3 %all-to-all-start = ((bf16[32,4,6144]{2,1,0:T(4,128)(2,1)}), bf16[32,4,6144]{2,1,0:T(4,128)(2,1)}, u32[]{:S(2)}, u32[]{:S(2)}) async-start(bf16[32,4,6144]{2,1,0:T(4,128)(2,1)} %stack.19), calls=%async_computation | async-start | bytes 3145728 | tf_op jit(solution)/shard_map/all_to_all | solution.py:47
  18.1 22.5 %all-to-all-done = bf16[32,4,6144]{2,1,0:T(4,128)(2,1)} async-done(((bf16[32,4,6144]{2,1,0:T(4,128)(2,1)}), bf16[32,4,6144]{2,1,0:T(4,128)(2,1)}, u32[]{:S(2)}, u32[]{:S(2)}) %all-to-all-start) | async-done | bytes 1572896 | tf_op jit(solution)/shard_map/all_to_all | solution.py:47
  40.6 3.6 %reshape.177 = bf16[128,6144]{1,0:T(8,128)(2,1)} reshape(bf16[32,4,6144]{2,1,0:T(4,128)(2,1)} %all-to-all-done) | data formatting | bytes 3145728 | tf_op jit(solution)/shard_map/reshape | solution.py:47
  44.2 3.6 %convolution_convert_fusion.3 = bf16[128,6144]{1,0:T(8,128)(2,1)} fusion(bf16[1,128,6144]{2,1,0:T(8,128)(2,1)S(1)} %copy-done, bf16[128,6144]{1,0:T(8,128)(2,1)} %reshape.177, bf16[1,6144,128]{2,1,0:T(8,128)(2,1)S(1)} %copy-done.1, f32[128]{0:T(128)S(1)} %get-tuple-element.12, f32[128]{0:T(128)S(1)} %bitcast_convert_fusion), kind=kOutput, calls=%fused_computation.3 | convolution fusion | flops 403505152 | bytes 6292480 | tf_op jit(solution)/shard_map/dot_general | solution.py:53
  47.9 3.8 %reshape.178 = bf16[32,4,6144]{2,1,0:T(4,128)(2,1)} reshape(bf16[128,6144]{1,0:T(8,128)(2,1)} %convolution_convert_fusion.3) | data formatting | bytes 3145728 | tf_op jit(solution)/shard_map/reshape | solution.py:56
  51.7 5.1 %all-to-all-start.1 = ((bf16[32,4,6144]{2,1,0:T(4,128)(2,1)}), bf16[32,4,6144]{2,1,0:T(4,128)(2,1)}, u32[]{:S(2)}, u32[]{:S(2)}) async-start(bf16[32,4,6144]{2,1,0:T(4,128)(2,1)} %reshape.178), calls=%async_computation.1 | async-start | bytes 3145728 | tf_op jit(solution)/shard_map/all_to_all | solution.py:57
  56.8 22.8 %all-to-all-done.1 = bf16[32,4,6144]{2,1,0:T(4,128)(2,1)} async-done(((bf16[32,4,6144]{2,1,0:T(4,128)(2,1)}), bf16[32,4,6144]{2,1,0:T(4,128)(2,1)}, u32[]{:S(2)}, u32[]{:S(2)}) %all-to-all-start.1) | async-done | bytes 1572896 | tf_op jit(solution)/shard_map/all_to_all | solution.py:57
  79.6 2.1 convert_reduce_fusion.3
  81.7 1.3 collective-permute-start
  83.0 1.2 collective-permute-done
  86.2 27.6 %all_to_all.40 = bf16[32,4,6144]{2,1,0:T(4,128)(2,1)} all-to-all(bf16[32,4,6144]{2,1,0:T(4,128)(2,1)S(1)} %stack.20), channel_id=1, replica_groups=mesh['pipe'=16,'blk'=32] {'blk'}, dimensions={0} | all-to-all | bytes 3145728 | tf_op jit(solution)/shard_map/all_to_all | solution.py:47
  113.8 3.7 %reshape.179 = bf16[128,6144]{1,0:T(8,128)(2,1)} reshape(bf16[32,4,6144]{2,1,0:T(4,128)(2,1)} %all_to_all.40) | data formatting | bytes 3145728 | tf_op jit(solution)/shard_map/reshape | solution.py:47
  117.5 3.6 %convolution_convert_fusion.2 = bf16[128,6144]{1,0:T(8,128)(2,1)} fusion(bf16[1,128,6144]{2,1,0:T(8,128)(2,1)S(1)} %copy-done, bf16[128,6144]{1,0:T(8,128)(2,1)} %reshape.179, bf16[1,6144,128]{2,1,0:T(8,128)(2,1)S(1)} %copy-done.1, f32[128]{0:T(128)S(1)} %get-tuple-element.11, f32[128]{0:T(128)S(1)} %bitcast_convert_fusion), kind=kOutput, calls=%fused_computation.2 | convolution fusion | flops 403505152 | bytes 6292480 | tf_op jit(solution)/shard_map/dot_general | solution.py:53
  121.1 3.8 %reshape.180 = bf16[32,4,6144]{2,1,0:T(4,128)(2,1)} reshape(bf16[128,6144]{1,0:T(8,128)(2,1)} %convolution_convert_fusion.2) | data formatting | bytes 3145728 | tf_op jit(solution)/shard_map/reshape | solution.py:56
  124.9 26.4 %all_to_all.41 = bf16[32,4,6144]{2,1,0:T(4,128)(2,1)S(1)} all-to-all(bf16[32,4,6144]{2,1,0:T(4,128)(2,1)} %reshape.180), channel_id=1, replica_groups=mesh['pipe'=16,'blk'=32] {'blk'}, dimensions={0} | all-to-all | bytes 3145728 | tf_op jit(solution)/shard_map/all_to_all | solution.py:57
  152.0 4.0 %collective-permute-start.1 = (bf16[4,6144]{1,0:T(4,128)(2,1)S(1)}, bf16[4,6144]{1,0:T(4,128)(2,1)S(1)}, u32[]{:S(2)}, u32[]{:S(2)}) collective-permute-start(bf16[4,6144]{1,0:T(4,128)(2,1)S(1)} %fusion.93), channel_id=1, source_target_pairs={{0,32},{32,64},{64,96},{96,128},{128,160},{160,192},{192,224},{224... | collective-permute-start | bytes 147464 | tf_op jit(solution)/shard_map/ppermute | solution.py:13
  156.0 1.3 collective-permute-done.1
  159.4 27.1 %all_to_all.42 = bf16[32,4,6144]{2,1,0:T(4,128)(2,1)} all-to-all(bf16[32,4,6144]{2,1,0:T(4,128)(2,1)S(1)} %stack.22), channel_id=1, replica_groups=mesh['pipe'=16,'blk'=32] {'blk'}, dimensions={0} | all-to-all | bytes 3145728 | tf_op jit(solution)/shard_map/all_to_all | solution.py:47
  186.4 3.7 %reshape.181 = bf16[128,6144]{1,0:T(8,128)(2,1)} reshape(bf16[32,4,6144]{2,1,0:T(4,128)(2,1)} %all_to_all.42) | data formatting | bytes 3145728 | tf_op jit(solution)/shard_map/reshape | solution.py:47
  190.1 3.6 %convolution_convert_fusion.1 = bf16[128,6144]{1,0:T(8,128)(2,1)} fusion(bf16[1,128,6144]{2,1,0:T(8,128)(2,1)S(1)} %copy-done, bf16[128,6144]{1,0:T(8,128)(2,1)} %reshape.181, bf16[1,6144,128]{2,1,0:T(8,128)(2,1)S(1)} %copy-done.1, f32[128]{0:T(128)S(1)} %get-tuple-element.10, f32[128]{0:T(128)S(1)} %bitcast_convert_fusion), kind=kOutput, calls=%fused_computation.1 | convolution fusion | flops 403505152 | bytes 6292480 | tf_op jit(solution)/shard_map/dot_general | solution.py:53
  193.7 3.8 %reshape.182 = bf16[32,4,6144]{2,1,0:T(4,128)(2,1)} reshape(bf16[128,6144]{1,0:T(8,128)(2,1)} %convolution_convert_fusion.1) | data formatting | bytes 3145728 | tf_op jit(solution)/shard_map/reshape | solution.py:56
  197.5 26.5 %all_to_all.43 = bf16[32,4,6144]{2,1,0:T(4,128)(2,1)S(1)} all-to-all(bf16[32,4,6144]{2,1,0:T(4,128)(2,1)} %reshape.182), channel_id=1, replica_groups=mesh['pipe'=16,'blk'=32] {'blk'}, dimensions={0} | all-to-all | bytes 3145728 | tf_op jit(solution)/shard_map/all_to_all | solution.py:57
  224.7 4.0 %collective-permute-start.2 = (bf16[4,6144]{1,0:T(4,128)(2,1)S(1)}, bf16[4,6144]{1,0:T(4,128)(2,1)S(1)}, u32[]{:S(2)}, u32[]{:S(2)}) collective-permute-start(bf16[4,6144]{1,0:T(4,128)(2,1)S(1)} %fusion.95), channel_id=1, source_target_pairs={{0,32},{32,64},{64,96},{96,128},{128,160},{160,192},{192,224},{224... | collective-permute-start | bytes 147464 | tf_op jit(solution)/shard_map/ppermute | solution.py:13
  228.7 1.3 collective-permute-done.2
  232.1 27.1 %all_to_all.44 = bf16[32,4,6144]{2,1,0:T(4,128)(2,1)} all-to-all(bf16[32,4,6144]{2,1,0:T(4,128)(2,1)S(1)} %stack.24), channel_id=1, replica_groups=mesh['pipe'=16,'blk'=32] {'blk'}, dimensions={0} | all-to-all | bytes 3145728 | tf_op jit(solution)/shard_map/all_to_all | solution.py:47
  259.1 3.7 %reshape.183 = bf16[128,6144]{1,0:T(8,128)(2,1)} reshape(bf16[32,4,6144]{2,1,0:T(4,128)(2,1)} %all_to_all.44) | data formatting | bytes 3145728 | tf_op jit(solution)/shard_map/reshape | solution.py:47
  262.8 3.6 %convolution_convert_fusion = bf16[128,6144]{1,0:T(8,128)(2,1)} fusion(bf16[1,128,6144]{2,1,0:T(8,128)(2,1)S(1)} %copy-done, bf16[128,6144]{1,0:T(8,128)(2,1)} %reshape.183, bf16[1,6144,128]{2,1,0:T(8,128)(2,1)S(1)} %copy-done.1, f32[128]{0:T(128)S(1)} %get-tuple-element.9, f32[128]{0:T(128)S(1)} %bitcast_convert_fusion), kind=kOutput, calls=%fused_computation | convolution fusion | flops 403505152 | bytes 6292480 | tf_op jit(solution)/shard_map/dot_general | solution.py:53
  266.4 3.8 %reshape.184 = bf16[32,4,6144]{2,1,0:T(4,128)(2,1)} reshape(bf16[128,6144]{1,0:T(8,128)(2,1)} %convolution_convert_fusion) | data formatting | bytes 3145728 | tf_op jit(solution)/shard_map/reshape | solution.py:56
  270.2 3.8 %all-to-all-start.7 = ((bf16[32,4,6144]{2,1,0:T(4,128)(2,1)}), bf16[32,4,6144]{2,1,0:T(4,128)(2,1)S(1)}, u32[]{:S(2)}, u32[]{:S(2)}) async-start(bf16[32,4,6144]{2,1,0:T(4,128)(2,1)} %reshape.184), calls=%async_computation.7 | async-start | bytes 3145728 | tf_op jit(solution)/shard_map/all_to_all | solution.py:57
  274.1 22.5 %all-to-all-done.7 = bf16[32,4,6144]{2,1,0:T(4,128)(2,1)S(1)} async-done(((bf16[32,4,6144]{2,1,0:T(4,128)(2,1)}), bf16[32,4,6144]{2,1,0:T(4,128)(2,1)S(1)}, u32[]{:S(2)}, u32[]{:S(2)}) %all-to-all-start.7) | async-done | bytes 1572896 | tf_op jit(solution)/shard_map/all_to_all | solution.py:57
  (54 shorter events, 12.9 us)
Async XLA Ops:
  0.0 44.2 %copy-start = (bf16[1,128,6144]{2,1,0:T(8,128)(2,1)S(1)}, bf16[1,128,6144]{2,1,0:T(8,128)(2,1)}, u32[]{:S(2)}) copy-start(bf16[1,128,6144]{2,1,0:T(8,128)(2,1)} %param.15) | copy-start | bytes 4718596
  6.4 11.3 %copy-start.4 = (s32[4,1,2,16]{3,2,1,0:T(2,128)S(1)}, s32[4,1,2,16]{3,2,1,0:T(2,128)}, u32[]{:S(2)}) copy-start(s32[4,1,2,16]{3,2,1,0:T(2,128)} %param.17) | copy-start | bytes 1540
  6.4 11.6 %copy-start.5 = (bf16[1,128]{1,0:T(2,128)(2,1)S(1)}, bf16[1,128]{1,0:T(2,128)(2,1)}, u32[]{:S(2)}) copy-start(bf16[1,128]{1,0:T(2,128)(2,1)} %param.14) | copy-start | bytes 772
  6.4 34.1 %all-to-all-start = ((bf16[32,4,6144]{2,1,0:T(4,128)(2,1)}), bf16[32,4,6144]{2,1,0:T(4,128)(2,1)}, u32[]{:S(2)}, u32[]{:S(2)}) async-start(bf16[32,4,6144]{2,1,0:T(4,128)(2,1)} %stack.19), calls=%async_computation | async-start | bytes 3145728 | tf_op jit(solution)/shard_map/all_to_all | solution.py:47
  18.1 26.1 %copy-start.1 = (bf16[1,6144,128]{2,1,0:T(8,128)(2,1)S(1)}, bf16[1,6144,128]{2,1,0:T(8,128)(2,1)}, u32[]{:S(2)}) copy-start(bf16[1,6144,128]{2,1,0:T(8,128)(2,1)} %param.13) | copy-start | bytes 4718596
  51.7 5.1 %copy-start.3 = (bf16[1,6144]{1,0:T(2,128)(2,1)S(1)}, bf16[1,6144]{1,0:T(2,128)(2,1)}, u32[]{:S(2)}) copy-start(bf16[1,6144]{1,0:T(2,128)(2,1)} %param.16) | copy-start | bytes 36868
  51.7 28.0 %all-to-all-start.1 = ((bf16[32,4,6144]{2,1,0:T(4,128)(2,1)}), bf16[32,4,6144]{2,1,0:T(4,128)(2,1)}, u32[]{:S(2)}, u32[]{:S(2)}) async-start(bf16[32,4,6144]{2,1,0:T(4,128)(2,1)} %reshape.178), calls=%async_computation.1 | async-start | bytes 3145728 | tf_op jit(solution)/shard_map/all_to_all | solution.py:57
  56.8 24.9 %copy-start.2 = (bf16[1,4,6144]{2,1,0:T(4,128)(2,1)S(1)}, bf16[1,4,6144]{2,1,0:T(4,128)(2,1)}, u32[]{:S(2)}) copy-start(bf16[1,4,6144]{2,1,0:T(4,128)(2,1)} %param.9) | copy-start | bytes 147460
  81.7 2.5 collective-permute-start
  152.0 5.3 %collective-permute-start.1 = (bf16[4,6144]{1,0:T(4,128)(2,1)S(1)}, bf16[4,6144]{1,0:T(4,128)(2,1)S(1)}, u32[]{:S(2)}, u32[]{:S(2)}) collective-permute-start(bf16[4,6144]{1,0:T(4,128)(2,1)S(1)} %fusion.93), channel_id=1, source_target_pairs={{0,32},{32,64},{64,96},{96,128},{128,160},{160,192},{192,224},{224... | collective-permute-start | bytes 147464 | tf_op jit(solution)/shard_map/ppermute | solution.py:13
  224.7 5.3 %collective-permute-start.2 = (bf16[4,6144]{1,0:T(4,128)(2,1)S(1)}, bf16[4,6144]{1,0:T(4,128)(2,1)S(1)}, u32[]{:S(2)}, u32[]{:S(2)}) collective-permute-start(bf16[4,6144]{1,0:T(4,128)(2,1)S(1)} %fusion.95), channel_id=1, source_target_pairs={{0,32},{32,64},{64,96},{96,128},{128,160},{160,192},{192,224},{224... | collective-permute-start | bytes 147464 | tf_op jit(solution)/shard_map/ppermute | solution.py:13
  270.2 26.3 %all-to-all-start.7 = ((bf16[32,4,6144]{2,1,0:T(4,128)(2,1)}), bf16[32,4,6144]{2,1,0:T(4,128)(2,1)S(1)}, u32[]{:S(2)}, u32[]{:S(2)}) async-start(bf16[32,4,6144]{2,1,0:T(4,128)(2,1)} %reshape.184), calls=%async_computation.7 | async-start | bytes 3145728 | tf_op jit(solution)/shard_map/all_to_all | solution.py:57
